TPU v7x, 256 devices: a whole 4x4x8 slice. The times are simulated.
256 devices in a mesh: segment: 2 (over core), expert: 32 (over y, z), tensor: 4 (over x).
Axes of the slice: x: 4, y: 4, z: 8, core: 2. Of those that a mesh axis runs over, the one named last changes fastest.
Arguments:
- activations: bfloat16 [2, 2048, 2560], P('segment', 'expert', 'tensor'), may hold values from -48 to 48
- expert_ids: int32 [2, 2048, 6], P(None, 'expert'), may hold values from 0 to 63, as said below
- route_weights: float32 [2, 2048, 6], P(None, 'expert'), may hold values from 0.05 to 1
- gain_dense: float32 [2560], replicated, may hold values from 0.25 to 1.75
- gain_expert: float32 [2560], replicated, may hold values from 0.25 to 1.75
- dense_gate: bfloat16 [2560, 6144], P('expert', 'tensor'), may hold values from -0.125 to 0.125
- dense_up: bfloat16 [2560, 6144], P('expert', 'tensor'), may hold values from -0.125 to 0.125
- dense_down: bfloat16 [2560, 6144], P('expert', 'tensor'), may hold values from -0.078125 to 0.078125
- expert_gate: bfloat16 [64, 2560, 1536], P('expert', None, 'tensor'), may hold values from -0.125 to 0.125
- expert_up: bfloat16 [64, 2560, 1536], P('expert', None, 'tensor'), may hold values from -0.125 to 0.125
- expert_down: bfloat16 [64, 1536, 2560], P('expert', 'tensor'), may hold values from -0.15625 to 0.15625
Outputs:
- sections: bfloat16 [2, 2, 2048, 2560], P('segment', None, 'expert', 'tensor')
Inputs may be any that keep to these rules, and one draw needn't show every extreme that they name: `expert_ids`: each token names 6 different experts. Split each micro-batch's tokens into blocks of 64 in order: no expert is named by more than 12 tokens of one block, and in every micro-batch one expert is named by exactly 12 tokens of every block.
All inputs are finite; a program needn't handle non-finite values.
Results may differ from a plain program's by a relative error of at most 0.009.
Values may be sent and summed in bfloat16 or wider, within the bound.
A program may use at most 128 MiB of HBM per device.

v0:
```python
import jax
import jax.numpy as jnp
from jax import lax
from jax.sharding import PartitionSpec as P

EPSILON = 1e-06


def shifted(block, axis, distance):
    devices = range(lax.axis_size(axis))
    route = [((i - distance) % len(devices), i) for i in devices]
    return lax.ppermute(block, axis, route)


def normalize(values, gain_row):
    inverse = lax.rsqrt(jnp.mean(values * values, axis=-1, keepdims=True) + EPSILON)
    return values * inverse * gain_row


def dense_prepare(micro_block, gain_dense):
    micro_count, tokens_here, quarter = micro_block.shape
    whole_rows = lax.all_gather(micro_block, "tensor", axis=2, tiled=True)
    full_width = whole_rows.shape[2]
    normed = normalize(whole_rows.astype(jnp.float32), gain_dense).astype(jnp.bfloat16)
    return normed.reshape(micro_count * tokens_here, full_width)


def dense_finish(micro_block, partial_value):
    micro_count, tokens_here, quarter = micro_block.shape
    summed = lax.psum_scatter(
        partial_value.reshape(micro_count, tokens_here, partial_value.shape[1]).astype(
            jnp.bfloat16
        ),
        "tensor",
        scatter_dimension=2,
        tiled=True,
    ).astype(jnp.float32)
    return (micro_block.astype(jnp.float32) + summed).astype(jnp.bfloat16)


def dense_folded(activations, gain_dense, dense_gate, dense_up, dense_down):
    normed = dense_prepare(activations, gain_dense)
    gate_sums = jnp.dot(
        normed,
        lax.all_gather(dense_gate, "expert", axis=0, tiled=True),
        preferred_element_type=jnp.float32,
    )
    upward = jnp.dot(
        normed,
        lax.all_gather(dense_up, "expert", axis=0, tiled=True),
        preferred_element_type=jnp.float32,
    )
    hidden = (jax.nn.silu(gate_sums) * upward).astype(jnp.bfloat16)
    partial_value = lax.dot_general(
        hidden,
        lax.all_gather(dense_down, "expert", axis=0, tiled=True),
        (((1,), (1,)), ((), ())),
        preferred_element_type=jnp.float32,
    )
    return dense_finish(activations, partial_value)


def route_slots(expert_ids_block, local_count, groups, capacity):
    tokens_here, picks = expert_ids_block.shape
    flat_ids = expert_ids_block.reshape(-1)
    experts_all = local_count * groups
    one_hot = (flat_ids[:, None] == jnp.arange(experts_all, dtype=jnp.int32)[None, :]).astype(
        jnp.int32
    )
    ranks = jnp.sum((jnp.cumsum(one_hot, axis=0) - 1) * one_hot, axis=1)
    slots = (flat_ids % local_count * groups + flat_ids // local_count) * capacity + ranks
    owners = jnp.arange(tokens_here * picks, dtype=jnp.int32) // picks
    sources = jnp.full((experts_all * capacity,), tokens_here, jnp.int32).at[slots].set(owners)
    return (slots, sources)


def place_rows(normed, sources, local_count, groups, capacity):
    padded = jnp.concatenate([normed, jnp.zeros((1, normed.shape[1]), normed.dtype)], axis=0)
    return padded[sources].reshape(local_count, groups, capacity, normed.shape[1])


def expert_block(
    middle, expert_ids_block, route_block, gain_expert, expert_gate, expert_up, expert_down
):
    tokens_here, quarter = middle.shape
    picks = expert_ids_block.shape[1]
    groups = lax.axis_size("expert")
    local_count, full_width, hidden_part = expert_gate.shape
    capacity = min(tokens_here, 2 * (tokens_here * picks // (local_count * groups)))
    slots, sources = route_slots(expert_ids_block, local_count, groups, capacity)
    middle_wide = middle.astype(jnp.float32)
    received_rows = groups * capacity
    tensor_index = lax.axis_index("tensor")
    square_sums = lax.psum(jnp.sum(middle_wide * middle_wide, axis=1), "tensor")
    inverse = lax.rsqrt(square_sums / full_width + EPSILON)
    gain_part = lax.dynamic_slice_in_dim(gain_expert, tensor_index * quarter, quarter, 0)
    normed = (middle_wide * inverse[:, None] * gain_part).astype(jnp.bfloat16)
    outgoing = place_rows(normed, sources, local_count, groups, capacity)
    arrived = lax.all_to_all(outgoing, "expert", split_axis=1, concat_axis=1, tiled=True)
    arrived = arrived.reshape(local_count, received_rows, quarter)
    slice_part = lax.all_gather(arrived, "tensor", axis=2, tiled=True)
    gate_sums = jnp.einsum(
        "lrc,lch->lrh", slice_part, expert_gate, preferred_element_type=jnp.float32
    )
    upward = jnp.einsum("lrc,lch->lrh", slice_part, expert_up, preferred_element_type=jnp.float32)
    hidden = (jax.nn.silu(gate_sums) * upward).astype(jnp.bfloat16)
    partial_value = jnp.einsum(
        "lrh,lhd->lrd", hidden, expert_down, preferred_element_type=jnp.float32
    )
    summed = lax.psum_scatter(
        partial_value.astype(jnp.bfloat16), "tensor", scatter_dimension=2, tiled=True
    )
    returned = lax.all_to_all(
        summed.reshape(local_count, groups, capacity, quarter),
        "expert",
        split_axis=1,
        concat_axis=1,
        tiled=True,
    )
    picked = returned.reshape(local_count * groups * capacity, quarter)[slots]
    picked = picked.reshape(tokens_here, picks, quarter).astype(jnp.float32)
    mixed = jnp.sum(route_block[:, :, None] * picked, axis=1)
    return (middle_wide + mixed).astype(jnp.bfloat16)


def body(
    activations,
    expert_ids,
    route_weights,
    gain_dense,
    gain_expert,
    dense_gate,
    dense_up,
    dense_down,
    expert_gate,
    expert_up,
    expert_down,
):
    segment_index = lax.axis_index("segment")
    own_middle = dense_folded(activations, gain_dense, dense_gate, dense_up, dense_down)
    other_middle = shifted(own_middle, "segment", 1)
    middles = jnp.where(
        segment_index == 0,
        jnp.concatenate([own_middle, other_middle], axis=0),
        jnp.concatenate([other_middle, own_middle], axis=0),
    )
    finals = jnp.stack(
        [
            expert_block(
                middles[position],
                expert_ids[position],
                route_weights[position],
                gain_expert,
                expert_gate,
                expert_up,
                expert_down,
            )
            for position in range(middles.shape[0])
        ]
    )
    sections = jnp.where(segment_index == 0, middles, finals)
    return sections[None]


def solution(mesh):
    placed = (
        P("segment", "expert", "tensor"),
        P(None, "expert", None),
        P(None, "expert", None),
        P(),
        P(),
        P("expert", "tensor"),
        P("expert", "tensor"),
        P("expert", "tensor"),
        P("expert", None, "tensor"),
        P("expert", None, "tensor"),
        P("expert", "tensor", None),
    )
    return jax.shard_map(
        body,
        mesh=mesh,
        in_specs=placed,
        out_specs=P("segment", None, "expert", "tensor"),
        check_vma=False,
    )
```

profile of v0, /device:TPU:32, one launch (start us, length us, event | category | flops | bytes accessed | tf_op | source)
XLA Modules:
  0.0 638.5 jit_solution(418148062136196478)
XLA Ops:
  11.0 13.0 %all_gather.18 = bf16[1,64,2560]{2,1,0:T(8,128)(2,1)S(1)} all-gather(bf16[1,64,640]{2,1,0:T(8,128)(2,1)} %param.11), channel_id=1, replica_groups=mesh['segment'=2,'expert'=32,'tensor'=4] {'tensor'}, dimensions={2}, use_global_device_ids=true | all-gather | bytes 409600 | tf_op jit(solution)/shard_map/all_gather | solution.py:22
  24.2 82.8 %all-gather.6.cloned.1.call-done = bf16[2560,1536]{1,0:T(8,128)(2,1)} async-done(((bf16[80,1536]{1,0:T(8,128)(2,1)}), bf16[2560,1536]{1,0:T(8,128)(2,1)}) %all-gather.6.cloned.1.call-update) | async-done | bytes 7864336 | tf_op jit(solution)/shard_map/all_gather | solution.py:45
  107.1 4.8 fusion.37
  111.9 90.8 %all-gather.10.cloned.1.call-done = bf16[2560,1536]{1,0:T(8,128)(2,1)} async-done(((bf16[80,1536]{1,0:T(8,128)(2,1)}), bf16[2560,1536]{1,0:T(8,128)(2,1)}) %all-gather.10.cloned.1.call-update) | async-done | bytes 7864336 | tf_op jit(solution)/shard_map/all_gather | solution.py:56
  202.7 95.6 %all-gather.8.cloned.1.call-done = bf16[2560,1536]{1,0:T(8,128)(2,1)} async-done(((bf16[80,1536]{1,0:T(8,128)(2,1)}), bf16[2560,1536]{1,0:T(8,128)(2,1)}) %all-gather.8.cloned.1.call-update) | async-done | bytes 7864336 | tf_op jit(solution)/shard_map/all_gather | solution.py:50
  298.3 9.4 %fusion = bf16[1,64,2560]{2,1,0:T(8,128)(2,1)S(1)} fusion(bf16[2560,1536]{1,0:T(8,128)(2,1)} %all-gather.10.cloned.1.call-done, bf16[2560,1536]{1,0:T(8,128)(2,1)} %all-gather.8.cloned.1.call-done, f32[64,1536]{1,0:T(8,128)S(1)} %fusion.37, bf16[1,64,2560]{2,1,0:T(8,128)(2,1)S(1)} %all_gather.18, f32[2560]{0:T(1024)S(1)} %copy-done.3, f32[64]{0:T(128)S(1)} %add_rsqrt_fusion.2), kind=kOutput, calls=%fused_computation.9 | convolution fusion | flops 1008041984 | bytes 16787712 | tf_op jit(solution)/shard_map/dot_general | solution.py:54
  314.3 18.2 %reduce-scatter.10.cloned.1.call-done = bf16[640,64]{1,0:T(8,128)(2,1)} async-done(((bf16[2560,64]{1,0:T(8,128)(2,1)}), bf16[640,64]{1,0:T(8,128)(2,1)}) %reduce-scatter.10.cloned.1.call-update) | async-done | bytes 81936
  336.0 8.4 %all-reduce.2 = (f32[64]{0:T(128)S(1)}, f32[64]{0:T(128)S(1)}) all-reduce(f32[64]{0:T(128)S(1)} %get-tuple-element.5, f32[64]{0:T(128)S(1)} %get-tuple-element.6), channel_id=1, replica_groups=mesh['segment'=2,'expert'=32,'tensor'=4] {'tensor'}, use_global_device_ids=true, to_apply=%region_3.4 | all-reduce | flops 128 | bytes 1024 | tf_op jit(solution)/shard_map/psum | solution.py:94
  348.6 35.7 %all_to_all.20 = bf16[2,32,12,640]{3,0,2,1:T(2,128)(2,1)S(1)} all-to-all(bf16[2,32,12,640]{3,0,2,1:T(2,128)(2,1)S(1)} %copy.50), channel_id=1, replica_groups=mesh['segment'=2,'expert'=32,'tensor'=4] {'expert'}, dimensions={1} | all-to-all | bytes 1966080 | tf_op jit(solution)/shard_map/all_to_all | solution.py:99
  395.1 29.5 %all_to_all.21 = bf16[2,32,12,640]{3,0,2,1:T(2,128)(2,1)S(1)} all-to-all(bf16[2,32,12,640]{3,0,2,1:T(2,128)(2,1)S(1)} %copy.40), channel_id=1, replica_groups=mesh['segment'=2,'expert'=32,'tensor'=4] {'expert'}, dimensions={1} | all-to-all | bytes 1966080 | tf_op jit(solution)/shard_map/all_to_all | solution.py:99
  428.7 5.5 fusion.60
  434.2 10.7 %convolution_convert_fusion = bf16[2,384,2560]{2,1,0:T(8,128)(2,1)} fusion(bf16[2,384,2560]{2,1,0:T(8,128)(2,1)} %param.21, bf16[2,384,2560]{2,1,0:T(8,128)(2,1)} %all-gather.14.cloned.1.call-done, bf16[2,2560,384]{2,1,0:T(8,128)(2,1)} %param.20, f32[2,384,384]{2,1,0:T(8,128)S(1)} %fusion.60), kind=kOutput, calls=%fused_computation.6 | convolution fusion | flops 3023634432 | bytes 16908288 | tf_op jit(solution)/shard_map/lrh,lhd->lrd/dot_general | solution.py:107
  444.8 10.6 %copy.58 = bf16[2,384,2560]{1,0,2:T(2,128)(2,1)} copy(bf16[2,384,2560]{2,1,0:T(8,128)(2,1)} %convolution_convert_fusion) | data formatting | bytes 7864320
  455.5 4.7 copy.70
  460.5 18.9 %all-gather.12.cloned.1.call-done = bf16[2,384,2560]{2,1,0:T(8,128)(2,1)} async-done(((bf16[2,384,640]{2,1,0:T(8,128)(2,1)}), bf16[2,384,2560]{2,1,0:T(8,128)(2,1)}) %all-gather.12.cloned.1.call-update) | async-done | bytes 3932176 | tf_op jit(solution)/shard_map/all_gather | solution.py:101
  479.4 5.5 fusion.59
  484.9 10.7 %convolution_convert_fusion.1 = bf16[2,384,2560]{2,1,0:T(8,128)(2,1)} fusion(bf16[2,384,2560]{2,1,0:T(8,128)(2,1)} %param.21, bf16[2,384,2560]{2,1,0:T(8,128)(2,1)} %all-gather.12.cloned.1.call-done, bf16[2,2560,384]{2,1,0:T(8,128)(2,1)} %param.20, f32[2,384,384]{2,1,0:T(8,128)S(1)} %fusion.59), kind=kOutput, calls=%fused_computation.7 | convolution fusion | flops 3023634432 | bytes 16908288 | tf_op jit(solution)/shard_map/lrh,lhd->lrd/dot_general | solution.py:107
  495.5 10.6 %copy.56 = bf16[2,384,2560]{1,0,2:T(2,128)(2,1)} copy(bf16[2,384,2560]{2,1,0:T(8,128)(2,1)} %convolution_convert_fusion.1) | data formatting | bytes 7864320
  506.1 4.7 copy.69
  510.8 18.7 %reduce-scatter.14.cloned.1.call-done = bf16[640,768]{1,0:T(8,128)(2,1)} async-done(((bf16[2560,768]{1,0:T(8,128)(2,1)}), bf16[640,768]{1,0:T(8,128)(2,1)}) %reduce-scatter.14.cloned.1.call-update) | async-done | bytes 983056
  534.6 10.2 %all-to-all-start.3 = ((bf16[2,32,12,640]{3,0,2,1:T(2,128)(2,1)}), bf16[2,32,12,640]{3,0,2,1:T(2,128)(2,1)S(1)}, u32[]{:S(2)}, u32[]{:S(2)}) async-start(bf16[2,32,12,640]{3,0,2,1:T(2,128)(2,1)} %bitcast.15), calls=%async_computation.3 | async-start | bytes 1966080 | tf_op jit(solution)/shard_map/all_to_all | solution.py:113
  544.9 34.2 %reduce-scatter.12.cloned.1.call-done = bf16[640,768]{1,0:T(8,128)(2,1)} async-done(((bf16[2560,768]{1,0:T(8,128)(2,1)}), bf16[640,768]{1,0:T(8,128)(2,1)}) %reduce-scatter.12.cloned.1.call-update) | async-done | bytes 983056
  584.2 10.1 %all-to-all-start.1 = ((bf16[2,32,12,640]{3,0,2,1:T(2,128)(2,1)}), bf16[2,32,12,640]{3,0,2,1:T(2,128)(2,1)S(1)}, u32[]{:S(2)}, u32[]{:S(2)}) async-start(bf16[2,32,12,640]{3,0,2,1:T(2,128)(2,1)} %bitcast.8), calls=%async_computation.1 | async-start | bytes 1966080 | tf_op jit(solution)/shard_map/all_to_all | solution.py:113
  600.7 20.8 %all-to-all-done.1 = bf16[2,32,12,640]{3,0,2,1:T(2,128)(2,1)S(1)} async-done(((bf16[2,32,12,640]{3,0,2,1:T(2,128)(2,1)}), bf16[2,32,12,640]{3,0,2,1:T(2,128)(2,1)S(1)}, u32[]{:S(2)}, u32[]{:S(2)}) %all-to-all-start.1) | async-done | bytes 983072 | tf_op jit(solution)/shard_map/all_to_all | solution.py:113
  (111 shorter events, 60.6 us)
Async XLA Ops:
  6.5 100.5 %all-gather.6.cloned.1.call-start = ((), (), s32[]{:S(2)}) async-start(), calls=%async_computation.7 | async-start | bytes 8110080 | tf_op jit(solution)/shard_map/all_gather | solution.py:45
  7.3 195.4 %all-gather.10.cloned.1.call-start = ((), (), s32[]{:S(2)}) async-start(), calls=%async_computation.9 | async-start | bytes 8110080 | tf_op jit(solution)/shard_map/all_gather | solution.py:56
  8.0 290.3 %all-gather.8.cloned.1.call-start = ((), (), s32[]{:S(2)}) async-start(), calls=%async_computation.8 | async-start | bytes 8110080 | tf_op jit(solution)/shard_map/all_gather | solution.py:50
  8.7 323.8 %reduce-scatter.10.cloned.1.call-start = ((), (), s32[]{:S(2)}) async-start(), calls=%async_computation.12 | async-start | bytes 819200
  24.2 274.0 %copy-start.3 = (f32[2560]{0:T(1024)S(1)}, f32[2560]{0:T(1024)}, u32[]{:S(2)}) copy-start(f32[2560]{0:T(1024)} %param.14) | copy-start | bytes 30724
  307.7 26.1 %copy-start.2 = (bf16[1,64,640]{2,1,0:T(8,128)(2,1)S(1)}, bf16[1,64,640]{2,1,0:T(8,128)(2,1)}, u32[]{:S(2)}) copy-start(bf16[1,64,640]{2,1,0:T(8,128)(2,1)} %param.11) | copy-start | bytes 245764
  309.6 119.1 %all-gather.14.cloned.1.call-start = ((), (), s32[]{:S(2)}) async-start(), calls=%async_computation.11 | async-start | bytes 4915200 | tf_op jit(solution)/shard_map/all_gather | solution.py:101
  310.8 0.6 copy-start.5
  333.8 1.4 collective-permute-start
  335.2 0.6 copy-start
  385.4 93.9 %all-gather.12.cloned.1.call-start = ((), (), s32[]{:S(2)}) async-start(), calls=%async_computation.10 | async-start | bytes 4915200 | tf_op jit(solution)/shard_map/all_gather | solution.py:101
  387.3 0.6 copy-start.7
  425.8 103.7 %reduce-scatter.14.cloned.1.call-start = ((), (), s32[]{:S(2)}) async-start(), calls=%async_computation.14 | async-start | bytes 4915200
  460.2 118.8 %reduce-scatter.12.cloned.1.call-start = ((), (), s32[]{:S(2)}) async-start(), calls=%async_computation.13 | async-start | bytes 4915200
  534.6 59.7 %copy-start.9 = (f32[2,64,6]{1,0,2:T(2,128)S(1)}, f32[2,64,6]{1,0,2:T(2,128)}, u32[]{:S(2)}) copy-start(f32[2,64,6]{1,0,2:T(2,128)} %param.13) | copy-start | bytes 9220
  534.6 60.5 %copy-start.6 = (s32[384]{0:T(512)S(1)}, s32[384]{0:T(512)}, u32[]{:S(2)}) copy-start(s32[384]{0:T(512)} %copy-done.5) | copy-start | bytes 4612
  534.6 61.1 %copy-start.8 = (s32[384]{0:T(512)S(1)}, s32[384]{0:T(512)}, u32[]{:S(2)}) copy-start(s32[384]{0:T(512)} %copy-done.7) | copy-start | bytes 4612
  534.6 49.6 %all-to-all-start.3 = ((bf16[2,32,12,640]{3,0,2,1:T(2,128)(2,1)}), bf16[2,32,12,640]{3,0,2,1:T(2,128)(2,1)S(1)}, u32[]{:S(2)}, u32[]{:S(2)}) async-start(bf16[2,32,12,640]{3,0,2,1:T(2,128)(2,1)} %bitcast.15), calls=%async_computation.3 | async-start | bytes 1966080 | tf_op jit(solution)/shard_map/all_to_all | solution.py:113
  584.2 37.3 %all-to-all-start.1 = ((bf16[2,32,12,640]{3,0,2,1:T(2,128)(2,1)}), bf16[2,32,12,640]{3,0,2,1:T(2,128)(2,1)S(1)}, u32[]{:S(2)}, u32[]{:S(2)}) async-start(bf16[2,32,12,640]{3,0,2,1:T(2,128)(2,1)} %bitcast.8), calls=%async_computation.1 | async-start | bytes 1966080 | tf_op jit(solution)/shard_map/all_to_all | solution.py:113
  624.9 4.1 copy-start.4
  624.9 6.0 copy-start.1
Sparse Core Ops, SparseCore 0:
  9.9 97.0 all-gather.5
  109.7 92.9 all-gather.9
  205.3 92.9 all-gather.7
  309.7 22.8 reduce-scatter.9
  385.6 43.0 all-gather.13
  430.4 48.9 all-gather.11
  481.9 47.5 reduce-scatter.13
  532.1 46.9 reduce-scatter.11
where the time goes:
time: 640 us; the launch traced here: 638 us
  waiting for transfers between devices  386 us (60%)
  blocking collectives  86.6 us (14%)
  local copies, waits for them, and re-layouts  77.5 us (12%)
  matrix products  46.4 us (7%)
  starting transfers between devices  20.9 us (3%)
  between operations  13.9 us (2%)
  other arithmetic  6.87 us (1%)
    all_gather x1, waiting for transfers between devices, dense_folded(): lax.all_gather(dense_up, 'expert', axis=0, tiled=True)  95.6 us
    all_gather x1, waiting for transfers between devices, dense_folded(): lax.all_gather(dense_down, 'expert', axis=0, tiled=True)  90.8 us
    all_gather x1, waiting for transfers between devices, dense_folded(): lax.all_gather(dense_gate, 'expert', axis=0, tiled=True)  82.8 us
    unnamed x11, waiting for transfers between devices  73.2 us
    all_to_all x2, blocking collectives, expert_block(): lax.all_to_all(outgoing, 'expert', split_axis=1, concat_axis=1, tiled=True)  65.2 us
    unnamed x30, local copies, waits for them, and re-layouts  40.2 us
    all_gather x2, waiting for transfers between devices, expert_block(): slice_part = lax.all_gather(arrived, 'tensor', axis=2, tiled=True)  21.7 us
    dot_general x2, matrix products, expert_block(): jnp.einsum('lrh,lhd->lrd', hidden, expert_down, preferred_element_type=jn...  21.3 us
  transfers between devices with their start and end apart: 11, of which 10 were waited for; matrix products, arithmetic and copies ran while one was open for 16% of the time, Pallas kernels for 0%

commit v1 on v0

--- a/solution.py
+++ b/solution.py
@@ -98,7 +98,40 @@
     outgoing = place_rows(normed, sources, local_count, groups, capacity)
     arrived = lax.all_to_all(outgoing, "expert", split_axis=1, concat_axis=1, tiled=True)
     arrived = arrived.reshape(local_count, received_rows, quarter)
-    slice_part = lax.all_gather(arrived, "tensor", axis=2, tiled=True)
+    x_now, right_arr, w_next = (
+        lax.psum(1, axis_name="tensor"),
+        lax.axis_index("tensor"),
+        arrived.shape[2],
+    )
+    table = []
+    for nth, s in enumerate(arrived.shape):
+        table.append(s * x_now if nth == 2 else s)
+    slice_part = lax.dynamic_update_slice_in_dim(
+        jnp.zeros(table, arrived.dtype), arrived, right_arr * w_next, axis=2
+    )
+    then = current_block = arrived
+    kk = 1
+    while kk < x_now // 2 + 1:
+        sheets = []
+        nth = 0
+        while nth < x_now:
+            sheets.append((nth, (nth + 1) % x_now))
+            nth += 1
+        then = lax.ppermute(then, axis_name="tensor", perm=sheets)
+        slice_part = lax.dynamic_update_slice_in_dim(
+            slice_part, then, (right_arr - kk) % x_now * w_next, axis=2
+        )
+        if 2 * kk < x_now:
+            made = []
+            nth = 0
+            while nth < x_now:
+                made.append((nth, (nth - 1) % x_now))
+                nth += 1
+            current_block = lax.ppermute(current_block, axis_name="tensor", perm=made)
+            slice_part = lax.dynamic_update_slice_in_dim(
+                slice_part, current_block, (right_arr + kk) % x_now * w_next, axis=2
+            )
+        kk = kk + 1
     gate_sums = jnp.einsum(
         "lrc,lch->lrh", slice_part, expert_gate, preferred_element_type=jnp.float32
     )

time: 640 us -> 690 us (1.078); the launches traced: 638 us -> 681 us
  waiting for transfers between devices: 386 us -> 421 us
  starting transfers between devices: 20.9 us -> 29.5 us
    ppermute x0 -> x6, waiting for transfers between devices: none -> 79.7 us  [the longest x4 79.7 us: expert_block(): then = lax.ppermute(then, axis_name='tensor', perm=sheets)]
    all_gather x2 -> x0, waiting for transfers between devices: 21.7 us -> none  [expert_block(): slice_part = lax.all_gather(arrived, 'tensor', axis=2, tiled=True)]
    unnamed x11 -> x9, waiting for transfers between devices: 73.2 us -> 52.7 us
    ppermute x0 -> x6, starting transfers between devices: none -> 8.38 us  [the longest x2 5.07 us: expert_block(): current_block = lax.ppermute(current_block, axis_name='tensor', perm=made)]
    unnamed x30 -> x38, local copies, waits for them, and re-layouts: 40.2 us -> 43 us
  transfers between devices with their start and end apart: 11 -> 15, of which waited for: 10 -> 11; matrix products, arithmetic and copies ran while one was open for 16% -> 10% of each run, Pallas kernels for 0% -> 0%
where the time goes in v1:
time: 690 us; the launch traced here: 681 us
  waiting for transfers between devices  421 us (61%)
  blocking collectives  88.2 us (13%)
  local copies, waits for them, and re-layouts  81.3 us (12%)
  matrix products  39.6 us (6%)
  starting transfers between devices  29.5 us (4%)
  between operations  14.3 us (2%)
    all_gather x1, waiting for transfers between devices, dense_folded(): lax.all_gather(dense_down, 'expert', axis=0, tiled=True)  95.6 us
    all_gather x1, waiting for transfers between devices, dense_folded(): lax.all_gather(dense_up, 'expert', axis=0, tiled=True)  90.8 us
    all_gather x1, waiting for transfers between devices, dense_folded(): lax.all_gather(dense_gate, 'expert', axis=0, tiled=True)  80.1 us
    ppermute x4, waiting for transfers between devices, expert_block(): then = lax.ppermute(then, axis_name='tensor', perm=sheets)  79.7 us
    all_to_all x2, blocking collectives, expert_block(): lax.all_to_all(outgoing, 'expert', split_axis=1, concat_axis=1, tiled=True)  66.8 us
    unnamed x9, waiting for transfers between devices  52.7 us
    unnamed x38, local copies, waits for them, and re-layouts  43 us
    dot_general x2, matrix products, expert_block(): jnp.einsum('lrh,lhd->lrd', hidden, expert_down, preferred_element_type=jn...  21.1 us
  transfers between devices with their start and end apart: 15, of which 11 were waited for; matrix products, arithmetic and copies ran while one was open for 10% of the time, Pallas kernels for 0%

profile of v1, /device:TPU:32, one launch (start us, length us, event | category | flops | bytes accessed | tf_op | source)
XLA Modules:
  0.0 680.5 jit_solution(17122669846106471444)
XLA Ops:
  13.8 13.0 %all_gather.12 = bf16[1,64,2560]{2,1,0:T(8,128)(2,1)S(1)} all-gather(bf16[1,64,640]{2,1,0:T(8,128)(2,1)} %param.11), channel_id=1, replica_groups=mesh['segment'=2,'expert'=32,'tensor'=4] {'tensor'}, dimensions={2}, use_global_device_ids=true | all-gather | bytes 409600 | tf_op jit(solution)/shard_map/all_gather | solution.py:22
  27.0 80.1 %all-gather.4.cloned.1.call-done = bf16[2560,1536]{1,0:T(8,128)(2,1)} async-done(((bf16[80,1536]{1,0:T(8,128)(2,1)}), bf16[2560,1536]{1,0:T(8,128)(2,1)}) %all-gather.4.cloned.1.call-update) | async-done | bytes 7864336 | tf_op jit(solution)/shard_map/all_gather | solution.py:45
  107.1 4.8 fusion.35
  111.9 90.8 %all-gather.6.cloned.1.call-done = bf16[2560,1536]{1,0:T(8,128)(2,1)} async-done(((bf16[80,1536]{1,0:T(8,128)(2,1)}), bf16[2560,1536]{1,0:T(8,128)(2,1)}) %all-gather.6.cloned.1.call-update) | async-done | bytes 7864336 | tf_op jit(solution)/shard_map/all_gather | solution.py:50
  202.7 95.6 %all-gather.8.cloned.1.call-done = bf16[2560,1536]{1,0:T(8,128)(2,1)} async-done(((bf16[80,1536]{1,0:T(8,128)(2,1)}), bf16[2560,1536]{1,0:T(8,128)(2,1)}) %all-gather.8.cloned.1.call-update) | async-done | bytes 7864336 | tf_op jit(solution)/shard_map/all_gather | solution.py:56
  298.3 9.4 %fusion = bf16[1,64,2560]{2,1,0:T(8,128)(2,1)S(1)} fusion(bf16[2560,1536]{1,0:T(8,128)(2,1)} %all-gather.8.cloned.1.call-done, bf16[2560,1536]{1,0:T(8,128)(2,1)} %all-gather.6.cloned.1.call-done, f32[64,1536]{1,0:T(8,128)S(1)} %fusion.35, bf16[1,64,2560]{2,1,0:T(8,128)(2,1)S(1)} %all_gather.12, f32[2560]{0:T(1024)S(1)} %copy-done.5, f32[64]{0:T(128)S(1)} %add_rsqrt_fusion.2), kind=kOutput, calls=%fused_computation.9 | convolution fusion | flops 1008041984 | bytes 16787712 | tf_op jit(solution)/shard_map/dot_general | solution.py:54
  312.9 19.7 %reduce-scatter.10.cloned.1.call-done = bf16[640,64]{1,0:T(8,128)(2,1)} async-done(((bf16[2560,64]{1,0:T(8,128)(2,1)}), bf16[640,64]{1,0:T(8,128)(2,1)}) %reduce-scatter.10.cloned.1.call-update) | async-done | bytes 81936
  336.0 8.4 %all-reduce.2 = (f32[64]{0:T(128)S(1)}, f32[64]{0:T(128)S(1)}) all-reduce(f32[64]{0:T(128)S(1)} %get-tuple-element.5, f32[64]{0:T(128)S(1)} %get-tuple-element.6), channel_id=1, replica_groups=mesh['segment'=2,'expert'=32,'tensor'=4] {'tensor'}, use_global_device_ids=true, to_apply=%region_3.4 | all-reduce | flops 128 | bytes 1024 | tf_op jit(solution)/shard_map/psum | solution.py:94
  348.6 35.6 %all_to_all.20 = bf16[2,32,12,640]{3,0,2,1:T(2,128)(2,1)S(1)} all-to-all(bf16[2,32,12,640]{3,0,2,1:T(2,128)(2,1)S(1)} %copy.59), channel_id=1, replica_groups=mesh['segment'=2,'expert'=32,'tensor'=4] {'expert'}, dimensions={1} | all-to-all | bytes 1966080 | tf_op jit(solution)/shard_map/all_to_all | solution.py:99
  387.5 18.2 %collective-permute-done.4 = bf16[2,384,640]{2,0,1:T(2,128)(2,1)S(1)} collective-permute-done((bf16[2,384,640]{2,0,1:T(2,128)(2,1)S(1)}, bf16[2,384,640]{2,0,1:T(2,128)(2,1)S(1)}, u32[]{:S(2)}, u32[]{:S(2)}) %collective-permute-start.4) | collective-permute-done | bytes 983072 | tf_op jit(solution)/shard_map/ppermute | solution.py:120
  408.4 17.1 %collective-permute-done.6 = bf16[2,384,640]{2,0,1:T(2,128)(2,1)} collective-permute-done((bf16[2,384,640]{2,0,1:T(2,128)(2,1)S(1)}, bf16[2,384,640]{2,0,1:T(2,128)(2,1)}, u32[]{:S(2)}, u32[]{:S(2)}) %collective-permute-start.6) | collective-permute-done | bytes 983072 | tf_op jit(solution)/shard_map/ppermute | solution.py:120
  431.0 10.5 %convolution_convert_fusion = bf16[2,384,2560]{2,1,0:T(8,128)(2,1)} fusion(bf16[2,384,2560]{2,1,0:T(8,128)(2,1)} %param.21, f32[2,384,384]{2,1,0:T(8,128)S(1)} %fusion.62, bf16[2,384,2560]{2,1,0:T(8,128)(2,1)} %copy-done.1, bf16[2,2560,384]{2,1,0:T(8,128)(2,1)} %param.20), kind=kOutput, calls=%fused_computation.6 | convolution fusion | flops 3023634432 | bytes 16908288 | tf_op jit(solution)/shard_map/lrh,lhd->lrd/dot_general | solution.py:140
  441.5 10.6 %copy.70 = bf16[2,384,2560]{1,0,2:T(2,128)(2,1)} copy(bf16[2,384,2560]{2,1,0:T(8,128)(2,1)} %convolution_convert_fusion) | data formatting | bytes 7864320
  452.1 4.7 copy.82
  463.9 31.1 %all_to_all.21 = bf16[2,32,12,640]{3,0,2,1:T(2,128)(2,1)S(1)} all-to-all(bf16[2,32,12,640]{3,0,2,1:T(2,128)(2,1)S(1)} %copy.46), channel_id=1, replica_groups=mesh['segment'=2,'expert'=32,'tensor'=4] {'expert'}, dimensions={1} | all-to-all | bytes 1966080 | tf_op jit(solution)/shard_map/all_to_all | solution.py:99
  498.3 22.5 %collective-permute-done.1 = bf16[2,384,640]{2,0,1:T(2,128)(2,1)S(1)} collective-permute-done((bf16[2,384,640]{2,0,1:T(2,128)(2,1)S(1)}, bf16[2,384,640]{2,0,1:T(2,128)(2,1)S(1)}, u32[]{:S(2)}, u32[]{:S(2)}) %collective-permute-start.1) | collective-permute-done | bytes 983072 | tf_op jit(solution)/shard_map/ppermute | solution.py:120
  521.9 21.9 %collective-permute-done.3 = bf16[2,384,640]{2,0,1:T(2,128)(2,1)S(1)} collective-permute-done((bf16[2,384,640]{2,0,1:T(2,128)(2,1)S(1)}, bf16[2,384,640]{2,0,1:T(2,128)(2,1)S(1)}, u32[]{:S(2)}, u32[]{:S(2)}) %collective-permute-start.3) | collective-permute-done | bytes 983072 | tf_op jit(solution)/shard_map/ppermute | solution.py:120
  548.2 10.6 %convolution_convert_fusion.1 = bf16[2,384,2560]{2,1,0:T(8,128)(2,1)} fusion(bf16[2,384,2560]{2,1,0:T(8,128)(2,1)} %param.21, f32[2,384,384]{2,1,0:T(8,128)S(1)} %fusion.61, bf16[2,384,2560]{2,1,0:T(8,128)(2,1)} %copy-done, bf16[2,2560,384]{2,1,0:T(8,128)(2,1)} %param.20), kind=kOutput, calls=%fused_computation.7 | convolution fusion | flops 3023634432 | bytes 16908288 | tf_op jit(solution)/shard_map/lrh,lhd->lrd/dot_general | solution.py:140
  558.8 10.8 %copy.68 = bf16[2,384,2560]{1,0,2:T(2,128)(2,1)} copy(bf16[2,384,2560]{2,1,0:T(8,128)(2,1)} %convolution_convert_fusion.1) | data formatting | bytes 7864320
  569.6 4.7 copy.81
  579.4 10.4 %all-to-all-start.3 = ((bf16[2,32,12,640]{3,0,2,1:T(2,128)(2,1)}), bf16[2,32,12,640]{3,0,2,1:T(2,128)(2,1)S(1)}, u32[]{:S(2)}, u32[]{:S(2)}) async-start(bf16[2,32,12,640]{3,0,2,1:T(2,128)(2,1)} %bitcast.15), calls=%async_computation.3 | async-start | bytes 1966080 | tf_op jit(solution)/shard_map/all_to_all | solution.py:146
  589.8 30.8 %reduce-scatter.12.cloned.1.call-done = bf16[640,768]{1,0:T(8,128)(2,1)} async-done(((bf16[2560,768]{1,0:T(8,128)(2,1)}), bf16[640,768]{1,0:T(8,128)(2,1)}) %reduce-scatter.12.cloned.1.call-update) | async-done | bytes 983056
  625.8 10.4 %all-to-all-start.1 = ((bf16[2,32,12,640]{3,0,2,1:T(2,128)(2,1)}), bf16[2,32,12,640]{3,0,2,1:T(2,128)(2,1)S(1)}, u32[]{:S(2)}, u32[]{:S(2)}) async-start(bf16[2,32,12,640]{3,0,2,1:T(2,128)(2,1)} %bitcast.8), calls=%async_computation.1 | async-start | bytes 1966080 | tf_op jit(solution)/shard_map/all_to_all | solution.py:146
  642.7 20.7 %all-to-all-done.1 = bf16[2,32,12,640]{3,0,2,1:T(2,128)(2,1)S(1)} async-done(((bf16[2,32,12,640]{3,0,2,1:T(2,128)(2,1)}), bf16[2,32,12,640]{3,0,2,1:T(2,128)(2,1)S(1)}, u32[]{:S(2)}, u32[]{:S(2)}) %all-to-all-start.1) | async-done | bytes 983072 | tf_op jit(solution)/shard_map/all_to_all | solution.py:146
  (132 shorter events, 73.8 us)
Async XLA Ops:
  6.5 100.5 %all-gather.4.cloned.1.call-start = ((), (), s32[]{:S(2)}) async-start(), calls=%async_computation.7 | async-start | bytes 8110080 | tf_op jit(solution)/shard_map/all_gather | solution.py:45
  7.3 195.4 %all-gather.6.cloned.1.call-start = ((), (), s32[]{:S(2)}) async-start(), calls=%async_computation.8 | async-start | bytes 8110080 | tf_op jit(solution)/shard_map/all_gather | solution.py:50
  8.0 290.3 %all-gather.8.cloned.1.call-start = ((), (), s32[]{:S(2)}) async-start(), calls=%async_computation.9 | async-start | bytes 8110080 | tf_op jit(solution)/shard_map/all_gather | solution.py:56
  8.7 323.8 %reduce-scatter.10.cloned.1.call-start = ((), (), s32[]{:S(2)}) async-start(), calls=%async_computation.10 | async-start | bytes 819200
  27.0 271.3 %copy-start.5 = (f32[2560]{0:T(1024)S(1)}, f32[2560]{0:T(1024)}, u32[]{:S(2)}) copy-start(f32[2560]{0:T(1024)} %param.14) | copy-start | bytes 30724
  307.7 26.1 %copy-start.4 = (bf16[1,64,640]{2,1,0:T(8,128)(2,1)S(1)}, bf16[1,64,640]{2,1,0:T(8,128)(2,1)}, u32[]{:S(2)}) copy-start(bf16[1,64,640]{2,1,0:T(8,128)(2,1)} %param.11) | copy-start | bytes 245764
  309.6 264.7 %reduce-scatter.14.cloned.1.call-start = ((), (), s32[]{:S(2)}) async-start(), calls=%async_computation.12 | async-start | bytes 4915200
  309.9 34.6 %copy-start.9 = (s32[384]{0:T(512)}, s32[384]{0:T(512)S(1)}, u32[]{:S(2)}) copy-start(s32[384]{0:T(512)S(1)} %get-tuple-element.18) | copy-start | bytes 4612
  309.9 146.9 %copy-start.7 = (s32[384]{0:T(512)}, s32[384]{0:T(512)S(1)}, u32[]{:S(2)}) copy-start(s32[384]{0:T(512)S(1)} %get-tuple-element.17) | copy-start | bytes 4612
  333.8 1.4 collective-permute-start
  384.2 21.5 %collective-permute-start.4 = (bf16[2,384,640]{2,0,1:T(2,128)(2,1)S(1)}, bf16[2,384,640]{2,0,1:T(2,128)(2,1)S(1)}, u32[]{:S(2)}, u32[]{:S(2)}) collective-permute-start(bf16[2,384,640]{2,0,1:T(2,128)(2,1)S(1)} %bitcast.117), channel_id=1, source_target_pairs={{0,1},{1,2},{2,3},{3,0},{4,5},{5,6},{6,7},{7,4},{8,9},{9,10},{10,1... | collective-permute-start | bytes 2949128 | tf_op jit(solution)/shard_map/ppermute | solution.py:120
  385.6 22.5 %collective-permute-start.5 = (bf16[2,384,640]{2,0,1:T(2,128)(2,1)S(1)}, bf16[2,384,640]{2,0,1:T(2,128)(2,1)S(1)}, u32[]{:S(2)}, u32[]{:S(2)}) collective-permute-start(bf16[2,384,640]{2,0,1:T(2,128)(2,1)S(1)} %bitcast.118), channel_id=1, source_target_pairs={{0,3},{1,0},{2,1},{3,2},{4,7},{5,4},{6,5},{7,6},{8,11},{9,8},{10,9... | collective-permute-start | bytes 2949128 | tf_op jit(solution)/shard_map/ppermute | solution.py:130
  405.7 19.7 %collective-permute-start.6 = (bf16[2,384,640]{2,0,1:T(2,128)(2,1)S(1)}, bf16[2,384,640]{2,0,1:T(2,128)(2,1)}, u32[]{:S(2)}, u32[]{:S(2)}) collective-permute-start(bf16[2,384,640]{2,0,1:T(2,128)(2,1)S(1)} %collective-permute-done.4), channel_id=1, source_target_pairs={{0,1},{1,2},{2,3},{3,0},{4,5},{5,6},{6,7},{7,4},{8,9},{9,10},{10,1... | collective-permute-start | bytes 2949128 | tf_op jit(solution)/shard_map/ppermute | solution.py:120
  407.7 21.0 %copy-start.12 = (bf16[2,2560,384]{2,1,0:T(8,128)(2,1)S(1)}, bf16[2,2560,384]{2,1,0:T(8,128)(2,1)}, u32[]{:S(2)}) copy-start(bf16[2,2560,384]{2,1,0:T(8,128)(2,1)} %param.19) | copy-start | bytes 11796484
  456.8 163.9 %reduce-scatter.12.cloned.1.call-start = ((), (), s32[]{:S(2)}) async-start(), calls=%async_computation.11 | async-start | bytes 4915200
  495.0 25.8 %collective-permute-start.1 = (bf16[2,384,640]{2,0,1:T(2,128)(2,1)S(1)}, bf16[2,384,640]{2,0,1:T(2,128)(2,1)S(1)}, u32[]{:S(2)}, u32[]{:S(2)}) collective-permute-start(bf16[2,384,640]{2,0,1:T(2,128)(2,1)S(1)} %bitcast.120), channel_id=1, source_target_pairs={{0,1},{1,2},{2,3},{3,0},{4,5},{5,6},{6,7},{7,4},{8,9},{9,10},{10,1... | collective-permute-start | bytes 2949128 | tf_op jit(solution)/shard_map/ppermute | solution.py:120
  495.0 26.6 %collective-permute-start.2 = (bf16[2,384,640]{2,0,1:T(2,128)(2,1)S(1)}, bf16[2,384,640]{2,0,1:T(2,128)(2,1)S(1)}, u32[]{:S(2)}, u32[]{:S(2)}) collective-permute-start(bf16[2,384,640]{2,0,1:T(2,128)(2,1)S(1)} %bitcast.121), channel_id=1, source_target_pairs={{0,3},{1,0},{2,1},{3,2},{4,7},{5,4},{6,5},{7,6},{8,11},{9,8},{10,9... | collective-permute-start | bytes 2949128 | tf_op jit(solution)/shard_map/ppermute | solution.py:130
  520.8 23.0 %collective-permute-start.3 = (bf16[2,384,640]{2,0,1:T(2,128)(2,1)S(1)}, bf16[2,384,640]{2,0,1:T(2,128)(2,1)S(1)}, u32[]{:S(2)}, u32[]{:S(2)}) collective-permute-start(bf16[2,384,640]{2,0,1:T(2,128)(2,1)S(1)} %collective-permute-done.1), channel_id=1, source_target_pairs={{0,1},{1,2},{2,3},{3,0},{4,5},{5,6},{6,7},{7,4},{8,9},{9,10},{10,1... | collective-permute-start | bytes 2949128 | tf_op jit(solution)/shard_map/ppermute | solution.py:120
  521.2 24.8 %copy-start.13 = (bf16[2,2560,384]{2,1,0:T(8,128)(2,1)S(1)}, bf16[2,2560,384]{2,1,0:T(8,128)(2,1)}, u32[]{:S(2)}) copy-start(bf16[2,2560,384]{2,1,0:T(8,128)(2,1)} %param.19) | copy-start | bytes 11796484
  579.4 56.8 %copy-start.11 = (f32[2,64,6]{1,0,2:T(2,128)S(1)}, f32[2,64,6]{1,0,2:T(2,128)}, u32[]{:S(2)}) copy-start(f32[2,64,6]{1,0,2:T(2,128)} %param.13) | copy-start | bytes 9220
  579.4 57.6 %copy-start.10 = (s32[384]{0:T(512)S(1)}, s32[384]{0:T(512)}, u32[]{:S(2)}) copy-start(s32[384]{0:T(512)} %copy-done.9) | copy-start | bytes 4612
  579.4 58.2 %copy-start.8 = (s32[384]{0:T(512)S(1)}, s32[384]{0:T(512)}, u32[]{:S(2)}) copy-start(s32[384]{0:T(512)} %copy-done.7) | copy-start | bytes 4612
  579.4 46.4 %all-to-all-start.3 = ((bf16[2,32,12,640]{3,0,2,1:T(2,128)(2,1)}), bf16[2,32,12,640]{3,0,2,1:T(2,128)(2,1)S(1)}, u32[]{:S(2)}, u32[]{:S(2)}) async-start(bf16[2,32,12,640]{3,0,2,1:T(2,128)(2,1)} %bitcast.15), calls=%async_computation.3 | async-start | bytes 1966080 | tf_op jit(solution)/shard_map/all_to_all | solution.py:146
  625.8 37.5 %all-to-all-start.1 = ((bf16[2,32,12,640]{3,0,2,1:T(2,128)(2,1)}), bf16[2,32,12,640]{3,0,2,1:T(2,128)(2,1)S(1)}, u32[]{:S(2)}, u32[]{:S(2)}) async-start(bf16[2,32,12,640]{3,0,2,1:T(2,128)(2,1)} %bitcast.8), calls=%async_computation.1 | async-start | bytes 1966080 | tf_op jit(solution)/shard_map/all_to_all | solution.py:146
  (5 other events, 14.6 us)
Sparse Core Ops, SparseCore 0:
  9.9 97.1 all-gather.3
  109.7 92.9 all-gather.5
  205.3 92.9 all-gather.7
  309.7 22.8 reduce-scatter.9
  456.9 48.3 reduce-scatter.13
  574.4 46.2 reduce-scatter.11
